TPU v7x, 128 devices: a whole 4x4x4 slice. The times are simulated.
128 devices in a mesh: wide: 32 (over y, z, core), narrow: 4 (over x).
Axes of the slice: x: 4, y: 4, z: 4, core: 2. Of those that a mesh axis runs over, the one named last changes fastest.
Arguments:
- field: bfloat16 [512, 2, 256, 1536], P('wide', None, None, 'narrow'), may hold values from -6 to 6
- table: bfloat16 [256, 1024, 1536], P('wide', None, 'narrow'), may hold values from -0.15625 to 0.15625
- inverse: bfloat16 [1024, 512, 512], P(('wide', 'narrow')), may hold values from -0.25 to 0.25
- modes: int32 [256], P('wide'), may hold values from 0 to 1023, as said below
Outputs:
- solved: float32 [1024, 2, 256, 512], P(('wide', 'narrow'))
Inputs may be any that keep to these rules, and one draw needn't show every extreme that they name: `modes`: each index of wide owns 4 * 2 consecutive slots; its slot i and slot i + 4 hold a pair m and 1023 - m with m < 512; no m is held twice.
All inputs are finite; a program needn't handle non-finite values.
Results may differ from a plain program's by a relative error of at most 0.013.
Values may be sent and summed in bfloat16 or wider, within the bound.
A program may use at most 128 MiB of HBM per device.

v0:
```python
import jax
import jax.numpy as jnp
from jax import lax
from jax.sharding import PartitionSpec as P


def per_device(field, table, inverse, modes):
    degree = lax.broadcasted_iota(jnp.int32, table.shape, 1)
    filtered_entries = jnp.where(degree >= modes[:, None, None], table, jnp.zeros_like(table))
    gathered = lax.all_to_all(field, "wide", split_axis=2, concat_axis=0, tiled=True)
    wide_count = lax.axis_size("wide")
    slim_mode_count = lax.axis_size("narrow")
    slots, degrees, width_block = filtered_entries.shape
    per_owner = degrees // (wide_count * slim_mode_count)
    reordered = filtered_entries.reshape(slots, wide_count, slim_mode_count, per_owner, width_block)
    reordered = jnp.transpose(reordered, (0, 2, 1, 3, 4)).reshape(slots, degrees, width_block)
    reduced_totals = lax.psum_scatter(
        jnp.einsum(
            "mlt,rcmt->lcmr", reordered, gathered, preferred_element_type=jnp.float32
        ).astype(jnp.bfloat16),
        "narrow",
        scatter_dimension=0,
        tiled=True,
    )
    harmonic_coefficient = reduced_totals
    harmonic_coefficient = lax.all_to_all(
        harmonic_coefficient, "wide", split_axis=0, concat_axis=2, tiled=True
    )
    return jnp.einsum(
        "etd,ebvd->ebvt", inverse, harmonic_coefficient, preferred_element_type=jnp.float32
    )


def solution(mesh):
    placed = (
        P("wide", None, None, "narrow"),
        P("wide", None, "narrow"),
        P(("wide", "narrow"), None, None),
        P("wide"),
    )
    return jax.shard_map(
        per_device,
        mesh=mesh,
        in_specs=placed,
        out_specs=P(("wide", "narrow"), None, None, None),
        check_vma=False,
    )
```

profile of v0, /device:TPU:19, one launch (start us, length us, event | category | flops | bytes accessed | tf_op | source)
XLA Modules:
  0.0 356.0 jit_solution(3216138822912776333)
XLA Ops:
  6.5 9.1 %copy.14 = bf16[16,2,256,384]{3,0,1,2:T(8,128)(2,1)} copy(bf16[16,2,256,384]{3,2,1,0:T(8,128)(2,1)} %param.4) | data formatting | bytes 12582912 | tf_op args[0]
  15.7 0.0 copy-start.1
  15.7 8.9 %all-to-all-start = ((bf16[16,2,256,384]{3,0,1,2:T(8,128)(2,1)}), bf16[16,2,256,384]{3,0,1,2:T(8,128)(2,1)}, u32[]{:S(2)}, u32[]{:S(2)}) async-start(bf16[16,2,256,384]{3,0,1,2:T(8,128)(2,1)} %copy.14), calls=%async_computation | async-start | bytes 12582912 | tf_op jit(solution)/shard_map/all_to_all | solution.py:10
  24.6 0.0 reduce-scatter.2.cloned.1.call-start
  24.7 0.0 copy-done.1
  24.7 5.3 %fusion = bf16[8,1024,384]{2,1,0:T(8,128)(2,1)S(1)} fusion(bf16[8,1024,384]{2,1,0:T(8,128)(2,1)} %param.5, s32[8]{0:T(128)S(1)} %copy-done.1), kind=kLoop, calls=%fused_computation.2 | loop fusion | flops 6291456 | bytes 12582944 | tf_op jit(solution)/shard_map/jit(_where)/select_n | solution.py:9
  30.0 3.8 %copy.13 = bf16[8,4,32,8,384]{4,3,2,1,0:T(8,128)(2,1)} copy(bf16[8,4,32,8,384]{4,3,1,2,0:T(8,128)(2,1)S(1)} %bitcast.28) | data formatting | bytes 12582912 | tf_op jit(solution)/shard_map/transpose | solution.py:16
  33.8 69.3 %all-to-all-done = bf16[16,2,256,384]{3,0,1,2:T(8,128)(2,1)} async-done(((bf16[16,2,256,384]{3,0,1,2:T(8,128)(2,1)}), bf16[16,2,256,384]{3,0,1,2:T(8,128)(2,1)}, u32[]{:S(2)}, u32[]{:S(2)}) %all-to-all-start) | async-done | bytes 6291488 | tf_op jit(solution)/shard_map/all_to_all | solution.py:10
  103.2 6.4 %copy.15 = bf16[16,2,32,8,384]{4,0,2,1,3:T(8,128)(2,1)} copy(bf16[16,2,32,8,384]{4,0,1,3,2:T(8,128)(2,1)} %bitcast.5) | data formatting | bytes 12582912 | tf_op jit(solution)/shard_map/all_to_all | solution.py:10
  109.6 16.1 %convert_bitcast_fusion = bf16[1024,2,8,512]{3,0,1,2:T(8,128)(2,1)} fusion(bf16[8,1024,384,1]{2,1,3,0:T(8,128)(2,1)} %bitcast.29, bf16[512,2,8,384]{3,0,1,2:T(8,128)(2,1)} %bitcast.30), kind=kOutput, calls=%fused_computation | convolution fusion | flops 6450839552 | bytes 29360128 | tf_op jit(solution)/shard_map/mlt,rcmt->lcmr/dot_general | solution.py:18
  125.6 0.0 reduce-scatter.2.cloned.1.call-update
  125.7 154.3 %reduce-scatter.2.cloned.1.call-done = bf16[256,2,8,512]{3,0,1,2:T(8,128)(2,1)} async-done(((bf16[1024,2,8,512]{3,0,1,2:T(8,128)(2,1)}), bf16[256,2,8,512]{3,0,1,2:T(8,128)(2,1)}) %reduce-scatter.2.cloned.1.call-update) | async-done | bytes 4194320 | tf_op jit(solution)/shard_map/reduce_scatter | solution.py:17
  279.9 6.6 %copy.16 = bf16[256,2,8,512]{3,1,2,0:T(2,128)(2,1)S(1)} copy(bf16[256,2,8,512]{3,0,1,2:T(8,128)(2,1)} %reduce-scatter.2.cloned.1.call-done) | data formatting | bytes 8388608 | tf_op jit(solution)/shard_map/reduce_scatter | solution.py:17
  286.5 0.0 copy-start
  286.5 56.9 %all_to_all.36 = bf16[256,2,8,512]{3,1,2,0:T(2,128)(2,1)S(1)} all-to-all(bf16[256,2,8,512]{3,1,2,0:T(2,128)(2,1)S(1)} %copy.16), channel_id=1, replica_groups=mesh['wide'=32,'narrow'=4] {'wide'}, dimensions={0} | all-to-all | bytes 8388608 | tf_op jit(solution)/shard_map/all_to_all | solution.py:26
  343.4 0.0 copy-done
  343.4 5.8 %fusion.1 = f32[8,2,256,512]{3,2,1,0:T(8,128)} fusion(bf16[8,512,512]{2,1,0:T(8,128)(2,1)S(1)} %copy-done, bf16[32,8,2,8,512]{4,2,3,1,0:T(2,128)(2,1)S(1)} %bitcast.27), kind=kOutput, calls=%fused_computation.3 | convolution fusion | flops 2147483648 | bytes 16777216 | tf_op jit(solution)/shard_map/etd,ebvd->ebvt/dot_general | solution.py:29
Async XLA Ops:
  15.7 9.0 %copy-start.1 = (s32[8]{0:T(128)S(1)}, s32[8]{0:T(128)}, u32[]{:S(2)}) copy-start(s32[8]{0:T(128)} %param.7) | copy-start | bytes 100
  15.7 87.5 %all-to-all-start = ((bf16[16,2,256,384]{3,0,1,2:T(8,128)(2,1)}), bf16[16,2,256,384]{3,0,1,2:T(8,128)(2,1)}, u32[]{:S(2)}, u32[]{:S(2)}) async-start(bf16[16,2,256,384]{3,0,1,2:T(8,128)(2,1)} %copy.14), calls=%async_computation | async-start | bytes 12582912 | tf_op jit(solution)/shard_map/all_to_all | solution.py:10
  24.6 255.3 %reduce-scatter.2.cloned.1.call-start = ((), (), s32[]{:S(2)}) async-start(), calls=%async_computation.3 | async-start | bytes 20971520 | tf_op jit(solution)/shard_map/reduce_scatter | solution.py:17
  286.5 56.9 %copy-start = (bf16[8,512,512]{2,1,0:T(8,128)(2,1)S(1)}, bf16[8,512,512]{2,1,0:T(8,128)(2,1)}, u32[]{:S(2)}) copy-start(bf16[8,512,512]{2,1,0:T(8,128)(2,1)} %param.6) | copy-start | bytes 12582916
Sparse Core Ops, SparseCore 0:
  125.8 154.0 reduce-scatter.1
where the time goes:
time: 360 us; the launch traced here: 356 us
  waiting for transfers between devices  224 us (62%)
  blocking collectives  56.9 us (16%)
  local copies, waits for them, and re-layouts  25.9 us (7%)
  matrix products  21.9 us (6%)
  between operations  13.4 us (4%)
  starting transfers between devices  8.98 us (2%)
  other arithmetic  5.32 us (1%)
    reduce_scatter x1, waiting for transfers between devices, per_device(): lax.psum_scatter(jnp.einsum('mlt,rcmt->lcmr', reordered, gathered, prefer...  154 us
    all_to_all x1, waiting for transfers between devices, per_device(): lax.all_to_all(field, 'wide', split_axis=2, concat_axis=0, tiled=True)  69.3 us
    all_to_all x1, blocking collectives, per_device(): lax.all_to_all(harmonic_coefficient, 'wide', split_axis=0, concat_axis=2,...  56.9 us
    dot_general x1, matrix products, per_device(): jnp.einsum('mlt,rcmt->lcmr', reordered, gathered, preferred_element_type=...  16.1 us
    unnamed x5, local copies, waits for them, and re-layouts  9.16 us
    all_to_all x1, starting transfers between devices, per_device(): lax.all_to_all(field, 'wide', split_axis=2, concat_axis=0, tiled=True)  8.94 us
  transfers between devices with their start and end apart: 2, of which 2 were waited for; matrix products, arithmetic and copies ran while one was open for 3% of the time, Pallas kernels for 0%

commit v1 on v0

v1 whole, which is shorter than its diff:
```python
import functools

import jax
import jax.numpy as jnp
from jax import lax
from jax.experimental import pallas as pl
from jax.experimental.pallas import tpu as pltpu
from jax.sharding import PartitionSpec as P

MESH = pl.DeviceIdType.MESH
BF16 = jnp.bfloat16
F32 = jnp.float32

WIDE = 32
NARROW = 4
CHIPS = 16
DEG = 1024
POS = 33
ROWS = POS * 64
NCH = 4
TB = 384

PLANE = [
    (0, 1), (1, 0), (0, 3), (3, 0), (1, 1), (3, 3), (1, 3), (3, 1),
    (0, 2), (2, 0), (1, 2), (2, 1), (3, 2), (2, 3), (2, 2),
]


def transform_kernel(
    field, table, modes, inverse,
    crecv, invt,
    arecv, tabv, modv, ft, res, pbuf, brecv, csend, invv, invo, perm,
    a_send, a_recv, t_sem, b_send, b_recv, c_send, c_recv, i_sem,
):
    w = lax.axis_index("wide")
    n = lax.axis_index("narrow")
    q = w // 2
    core = w % 2
    y = q // 4
    z = q % 4
    sib = w + 1 - 2 * core

    own_table = pltpu.make_async_copy(table, tabv.at[core], t_sem.at[0])
    own_table.start()
    own_modes = pltpu.make_async_copy(modes, modv.at[core], t_sem.at[1])
    own_modes.start()
    inv_in = pltpu.make_async_copy(inverse, invv, i_sem.at[0])
    inv_in.start()
    for k in range(NCH):
        pltpu.make_async_copy(
            field.at[pl.ds(8 * (k % 2), 8), k // 2, q], arecv.at[k, q], a_recv.at[k]
        ).start()

    barrier = pltpu.get_barrier_semaphore()

    def greet(t, carry):
        pl.semaphore_signal(
            barrier, inc=1, device_id=(lax.rem(w + t, WIDE), n), device_id_type=MESH
        )
        return carry

    lax.fori_loop(1, WIDE, greet, 0)
    for d in range(1, NARROW):
        pl.semaphore_signal(
            barrier, inc=1, device_id=(w, lax.rem(n + d, NARROW)), device_id_type=MESH
        )
    pl.semaphore_wait(barrier, WIDE - 1 + NARROW - 1)

    def send_field(k):
        for dy, dz in PLANE:
            peer = lax.rem(y + dy, 4) * 4 + lax.rem(z + dz, 4)
            pltpu.make_async_remote_copy(
                src_ref=field.at[pl.ds(8 * (k % 2), 8), k // 2, peer],
                dst_ref=arecv.at[k, q],
                send_sem=a_send.at[k],
                recv_sem=a_recv.at[k],
                device_id=(peer * 2 + core, n),
                device_id_type=MESH,
            ).start()

    give_modes = pltpu.make_async_remote_copy(
        src_ref=modes, dst_ref=modv.at[core], send_sem=t_sem.at[2],
        recv_sem=t_sem.at[3], device_id=(sib, n), device_id_type=MESH,
    )
    give_modes.start()
    give_table = pltpu.make_async_remote_copy(
        src_ref=table, dst_ref=tabv.at[core], send_sem=t_sem.at[4],
        recv_sem=t_sem.at[5], device_id=(sib, n), device_id_type=MESH,
    )
    send_field(0)
    give_table.start()
    send_field(1)

    inv_in.wait()
    arrive = lax.broadcasted_iota(jnp.int32, (512, 512), 0)
    natural = (
        ((arrive // 8) % 16) * 32 + (arrive // 256) * 16 + ((arrive // 128) % 2) * 8 + arrive % 8
    )
    radius = lax.broadcasted_iota(jnp.int32, (512, 512), 1)
    perm[...] = jnp.where(radius == natural, 1.0, 0.0).astype(BF16)

    def reorder(t, carry):
        invo[t] = lax.dot_general(
            perm[...], invv[t], (((1,), (1,)), ((), ())), preferred_element_type=F32
        ).astype(BF16)
        return carry

    lax.fori_loop(0, 8, reorder, 0)
    inv_out = pltpu.make_async_copy(invo, invt, i_sem.at[1])
    inv_out.start()

    own_table.wait()
    own_modes.wait()
    give_modes.wait()
    give_table.wait()

    def transform(k):
        whole = arecv.at[k]
        pltpu.make_async_copy(whole, whole, a_recv.at[k]).wait()
        if k + 2 < NCH:
            send_field(k + 2)

        def turn(t, carry):
            block = arecv[k, pl.ds(2 * t, 2)].reshape(16, 16, TB)
            ft[:, pl.ds(pl.multiple_of(16 * t, 16), 16), :] = jnp.swapaxes(block, 0, 1)
            return carry

        lax.fori_loop(0, 8, turn, 0)

        def two_pairs(pp, carry):
            side = pp // 2
            first = 2 * (pp % 2)
            for e in range(2):
                for kind in range(2):
                    slot = first + e + 4 * kind

                    def rows(b, c2):
                        at = pl.ds(pl.multiple_of(b * 256, 256), 256)
                        res[e, kind, at, :] = lax.dot_general(
                            tabv[side, slot, at, :], ft[side * 8 + slot],
                            (((1,), (1,)), ((), ())), preferred_element_type=F32,
                        )
                        return c2

                    lax.fori_loop(0, DEG // 256, rows, 0)

            at32 = lax.broadcasted_iota(jnp.int32, (32, 128), 0)

            def part(e, kind, block):
                rows = res[e, kind, pl.ds(pl.multiple_of(block * 32, 32), 32), :]
                m = modv[side, pl.ds(first + e + 4 * kind, 1), :]
                return jnp.where(at32 + block * 32 >= m, rows, 0.0)

            def put(pos, vals):
                for t in range(NARROW):
                    both = jnp.concatenate([v[8 * t:8 * t + 8] for v in vals], axis=0)
                    pbuf[k, t, pl.ds(pl.multiple_of(pos * 64 + pp * 16, 16), 16), :] = (
                        both.astype(BF16)
                    )

            put(0, [part(e, 1, 31) for e in range(2)])
            put(32, [part(e, 0, 31) for e in range(2)])

            def fold(v, c2):
                put(v + 1, [part(e, 0, v) + part(e, 1, 30 - v) for e in range(2)])
                return c2

            lax.fori_loop(0, 31, fold, 0)
            return carry

        lax.fori_loop(0, 4, two_pairs, 0)
        for d in range(1, NARROW):
            to = lax.rem(n + d, NARROW)
            pltpu.make_async_remote_copy(
                src_ref=pbuf.at[k, to], dst_ref=brecv.at[k, d - 1],
                send_sem=b_send.at[k], recv_sem=b_recv.at[k],
                device_id=(w, to), device_id_type=MESH,
            ).start()

    def spectral(k):
        whole = brecv.at[k]
        pltpu.make_async_copy(whole, whole, b_recv.at[k]).wait()

        def modes_of(kind):
            return jnp.concatenate(
                [modv[s, 4 * kind:4 * kind + 4, :] for s in range(2)], axis=0
            )

        lo_modes, hi_modes = modes_of(0), modes_of(1)
        at = lax.broadcasted_iota(jnp.int32, (8, 8, 128), 0)

        def put(pos, v, kind, m):
            rows = pl.ds(pl.multiple_of(pos * 64, 64), 64)
            total = pbuf[k, n, rows, :].astype(F32)
            for d in range(NARROW - 1):
                total = total + brecv[k, d, rows, :].astype(F32)
            turned = jnp.swapaxes(total.reshape(8, 8, 128), 0, 1)
            kept = jnp.where(at + (v * 32 + n * 8) >= m[None], turned, 0.0)
            csend[k, 2 * v + kind] = kept.reshape(64, 128).astype(BF16)

        def low(v, carry):
            put(v + 1, v, 0, lo_modes)
            return carry

        def high(v, carry):
            put(31 - v, v, 1, hi_modes)
            return carry

        lax.fori_loop(0, WIDE, low, 0)
        lax.fori_loop(WIDE // 2, WIDE, high, 0)

        @pl.when(w >= WIDE // 2)
        def _():
            pltpu.make_async_copy(
                csend.at[k, pl.ds(2 * w, 2)], crecv.at[k, pl.ds(2 * w, 2)], c_recv.at[k]
            ).start()

        @pl.when(w < WIDE // 2)
        def _():
            pltpu.make_async_copy(
                csend.at[k, pl.ds(2 * w, 1)], crecv.at[k, pl.ds(2 * w, 1)], c_recv.at[k]
            ).start()

        def give(t, carry):
            to = lax.rem(w + t, WIDE)

            def go(count):
                pltpu.make_async_remote_copy(
                    src_ref=csend.at[k, pl.ds(2 * to, count)],
                    dst_ref=crecv.at[k, pl.ds(2 * w, count)],
                    send_sem=c_send.at[k], recv_sem=c_recv.at[k],
                    device_id=(to, n), device_id_type=MESH,
                ).start()

            @pl.when(to >= WIDE // 2)
            def _():
                go(2)

            @pl.when(to < WIDE // 2)
            def _():
                go(1)

            return carry

        lax.fori_loop(1, WIDE, give, 0)

    for k in range(NCH):
        transform(k)
        if k:
            spectral(k - 1)
    spectral(NCH - 1)

    def drain(ref, sem):
        pltpu.make_async_copy(ref, ref, sem).wait()

    for k in range(NCH):
        drain(arecv.at[k, pl.ds(0, 15)], a_send.at[k])
        drain(brecv.at[k], b_send.at[k])

        @pl.when(w >= WIDE // 2)
        def _():
            drain(csend.at[k, pl.ds(0, 46)], c_send.at[k])
            drain(crecv.at[k], c_recv.at[k])

        @pl.when(w < WIDE // 2)
        def _():
            drain(csend.at[k, pl.ds(0, 47)], c_send.at[k])
            drain(crecv.at[k, pl.ds(0, 32)], c_recv.at[k])
    inv_out.wait()


def solve_kernel(where, x_ref, inv_ref, out_ref):
    keep = where[0] >= WIDE // 2
    vals = x_ref[...].astype(F32)
    lane = vals.reshape(2, CHIPS, 2, 2, 2, 8, 128)
    for e in range(2):
        blocks = []
        for half in range(2):
            for g in range(2):
                lo = lane[g, :, half, 0, e]
                hi = jnp.where(keep, lane[g, :, half, 1, e], 0.0)
                both = jnp.stack([lo, hi], axis=1)
                blocks.append(both.reshape(CHIPS * 16, 128).astype(BF16))
        lhs = jnp.concatenate(blocks, axis=1)
        got = jnp.dot(lhs, inv_ref[e], preferred_element_type=F32)
        got = got.reshape(CHIPS, 2, 8, 512)
        lo, hi = got[:, 0], got[:, 1]
        first = jnp.concatenate([lo[:, :4], hi[:, :4]], axis=1)
        second = jnp.concatenate([lo[:, 4:], hi[:, 4:]], axis=1)
        out_ref[e, 0] = jnp.stack([first, second], axis=1).reshape(256, 512)


def per_device(field, table, inverse, modes):
    fields = field.reshape(16, 2, CHIPS, 16, TB)
    modes_rows = jnp.broadcast_to(modes[:, None], (8, 128))
    any_spec = pl.BlockSpec(memory_space=pl.ANY)
    vmem_spec = pl.BlockSpec(memory_space=pltpu.VMEM)
    dma = pltpu.SemaphoreType.DMA
    crecv, invt = pl.pallas_call(
        transform_kernel,
        name="transform",
        out_shape=(
            jax.ShapeDtypeStruct((NCH, 2 * WIDE, 64, 128), BF16),
            jax.ShapeDtypeStruct((8, 512, 512), BF16),
        ),
        in_specs=[any_spec, any_spec, vmem_spec, any_spec],
        out_specs=(any_spec, any_spec),
        scratch_shapes=[
            pltpu.VMEM((NCH, CHIPS, 8, 16, TB), BF16),
            pltpu.VMEM((2, 8, DEG, TB), BF16),
            pltpu.VMEM((2, 8, 128), jnp.int32),
            pltpu.VMEM((16, 128, TB), BF16),
            pltpu.VMEM((2, 2, DEG, 128), F32),
            pltpu.VMEM((NCH, NARROW, ROWS, 128), BF16),
            pltpu.VMEM((NCH, NARROW - 1, ROWS, 128), BF16),
            pltpu.VMEM((NCH, 2 * WIDE, 64, 128), BF16),
            pltpu.VMEM((8, 512, 512), BF16),
            pltpu.VMEM((8, 512, 512), BF16),
            pltpu.VMEM((512, 512), BF16),
            dma((NCH,)), dma((NCH,)), dma((6,)), dma((NCH,)), dma((NCH,)),
            dma((NCH,)), dma((NCH,)), dma((2,)),
        ],
        compiler_params=pltpu.CompilerParams(
            collective_id=0, has_side_effects=True, vmem_limit_bytes=60 * 2**20
        ),
    )(fields, table, modes_rows, inverse)
    x = crecv.reshape(NCH, CHIPS, 2, 2, 64, 128)
    where = lax.axis_index("wide").astype(jnp.int32).reshape(1)
    return pl.pallas_call(
        solve_kernel,
        name="solve",
        out_shape=jax.ShapeDtypeStruct((8, 2, 256, 512), F32),
        grid_spec=pltpu.PrefetchScalarGridSpec(
            num_scalar_prefetch=1,
            grid=(4, 2),
            in_specs=[
                pl.BlockSpec((2, CHIPS, 2, 2, 16, 128), lambda i, c, s: (c, 0, 0, 0, i, 0)),
                pl.BlockSpec((2, 512, 512), lambda i, c, s: (i, 0, 0)),
            ],
            out_specs=pl.BlockSpec((2, 1, 256, 512), lambda i, c, s: (i, c, 0, 0)),
        ),
        compiler_params=pltpu.CompilerParams(vmem_limit_bytes=48 * 2**20),
    )(where, x, invt)


def solution(mesh):
    placed = (
        P("wide", None, None, "narrow"),
        P("wide", None, "narrow"),
        P(("wide", "narrow"), None, None),
        P("wide"),
    )
    return jax.shard_map(
        per_device,
        mesh=mesh,
        in_specs=placed,
        out_specs=P(("wide", "narrow"), None, None, None),
        check_vma=False,
    )
```

time: 360 us -> 172 us (0.48)
  waiting for transfers between devices: 224 us -> 0 us
  Pallas kernels: 0 us -> 165 us
  blocking collectives: 56.9 us -> 0 us
  local copies, waits for them, and re-layouts: 25.9 us -> 3.5 us
  matrix products: 21.9 us -> 0 us
  between operations: 13.4 us -> 0.02 us
  starting transfers between devices: 8.98 us -> 0 us
  other arithmetic: 5.32 us -> 0 us
    pallas_call x0 -> x2, Pallas kernels: none -> 165 us  [the longest x1 154 us: per_device(): pl.pallas_call(transform_kernel, name='transform', out_shape=(jax.ShapeDt...]
    reduce_scatter x1 -> x0, waiting for transfers between devices: 154 us -> none  [per_device(): lax.psum_scatter(jnp.einsum('mlt,rcmt->lcmr', reordered, gathered, prefer...]
    all_to_all x1 -> x0, waiting for transfers between devices: 69.3 us -> none  [per_device(): lax.all_to_all(field, 'wide', split_axis=2, concat_axis=0, tiled=True)]
    all_to_all x1 -> x0, blocking collectives: 56.9 us -> none  [per_device(): lax.all_to_all(harmonic_coefficient, 'wide', split_axis=0, concat_axis=2,...]
    dot_general x2 -> x0, matrix products: 21.9 us -> none  [the longest x1 16.1 us: per_device(): jnp.einsum('mlt,rcmt->lcmr', reordered, gathered, preferred_element_type=...]
    all_to_all x1 -> x0, starting transfers between devices: 8.94 us -> none  [per_device(): lax.all_to_all(field, 'wide', split_axis=2, concat_axis=0, tiled=True)]
    unnamed x5 -> x2, local copies, waits for them, and re-layouts: 9.16 us -> 2.18 us
    reduce_scatter x1 -> x0, local copies, waits for them, and re-layouts: 6.56 us -> none  [per_device(): lax.psum_scatter(jnp.einsum('mlt,rcmt->lcmr', reordered, gathered, prefer...]
  transfers between devices with their start and end apart: 2 -> 0, of which waited for: 2 -> 0; matrix products, arithmetic and copies ran while one was open for 3% -> 0% of each run, Pallas kernels for 0% -> 0%
where the time goes in v1:
time: 172 us; the launch traced here: 168 us
  Pallas kernels  165 us (96%)
  local copies, waits for them, and re-layouts  3.5 us (2%)
    pallas_call x1, Pallas kernels, per_device(): pl.pallas_call(transform_kernel, name='transform', out_shape=(jax.ShapeDt...  154 us
    pallas_call x1, Pallas kernels, per_device(): pl.pallas_call(solve_kernel, name='solve', out_shape=jax.ShapeDtypeStruct...  10.5 us

profile of v1, /device:TPU:19, one launch (start us, length us, event | category | flops | bytes accessed | tf_op | source)
XLA Modules:
  0.0 168.2 jit_solution(12640609174391561286)
XLA Ops:
  0.0 1.3 broadcast_in_dim.2.modes
  1.3 154.2 %transform.1 = (bf16[4,64,64,128]{3,2,1,0:T(8,128)(2,1)}, bf16[8,512,512]{2,1,0:T(8,128)(2,1)}) custom-call(bf16[16,2,16,16,384]{4,3,2,1,0:T(8,128)(2,1)} %bitcast.4, bf16[8,1024,384]{2,1,0:T(8,128)(2,1)} %table.1, s32[8,128]{1,0:T(8,128)} %broadcast_in_dim.2.modes, bf16[8,512,512]{2,1,0:T(8,128)(2,1)} %inverse.1), custom_call_target="tpu_custom_call" | custom-call | tf_op jit(solution)/shard_map/transform/pallas_call | solution.py:299
  155.5 0.0 copy-start
  155.5 2.2 %copy-done = bf16[4,64,64,128]{3,2,1,0:T(8,128)(2,1)S(1)} copy-done((bf16[4,64,64,128]{3,2,1,0:T(8,128)(2,1)S(1)}, bf16[4,64,64,128]{3,2,1,0:T(8,128)(2,1)}, u32[]{:S(2)}) %copy-start) | copy-done | bytes 4194328
  157.7 10.5 %solve.1 = f32[8,2,256,512]{3,2,1,0:T(8,128)} custom-call(s32[1]{0:T(128)} %bitcast.where, bf16[4,16,2,2,64,128]{5,4,3,2,1,0:T(8,128)(2,1)S(1)} %bitcast.3, bf16[8,512,512]{2,1,0:T(8,128)(2,1)} %get-tuple-element.8.inv_ref), custom_call_target="tpu_custom_call" | custom-call | tf_op jit(solution)/shard_map/solve/pallas_call | solution.py:329
Async XLA Ops:
  155.5 2.2 %copy-start = (bf16[4,64,64,128]{3,2,1,0:T(8,128)(2,1)S(1)}, bf16[4,64,64,128]{3,2,1,0:T(8,128)(2,1)}, u32[]{:S(2)}) copy-start(bf16[4,64,64,128]{3,2,1,0:T(8,128)(2,1)} %get-tuple-element.7) | copy-start | bytes 12582916

commit v2 on v1

--- a/solution.py
+++ b/solution.py
@@ -17,6 +17,7 @@
 DEG = 1024
 POS = 33
 ROWS = POS * 64
+HALF = ROWS // 2
 NCH = 4
 TB = 384
 
@@ -29,7 +30,7 @@
 def transform_kernel(
     field, table, modes, inverse,
     crecv, invt,
-    arecv, tabv, modv, ft, res, pbuf, brecv, csend, invv, invo, perm,
+    arecv, tabv, modv, ft, res, pbuf, brecv, bpass, csend, invv, invo, perm,
     a_send, a_recv, t_sem, b_send, b_recv, c_send, c_recv, i_sem,
 ):
     w = lax.axis_index("wide")
@@ -114,9 +115,19 @@
     give_modes.wait()
     give_table.wait()
 
+    right, opposite, left = (lax.rem(n + d, NARROW) for d in range(1, NARROW))
+
+    def landed(ref, sem):
+        pltpu.make_async_copy(ref, ref, sem).wait()
+
+    def hop(src, dst, to, send_sem, recv_sem):
+        pltpu.make_async_remote_copy(
+            src_ref=src, dst_ref=dst, send_sem=send_sem, recv_sem=recv_sem,
+            device_id=(w, to), device_id_type=MESH,
+        ).start()
+
     def transform(k):
-        whole = arecv.at[k]
-        pltpu.make_async_copy(whole, whole, a_recv.at[k]).wait()
+        landed(arecv.at[k], a_recv.at[k])
         if k + 2 < NCH:
             send_field(k + 2)
 
@@ -133,16 +144,10 @@
             for e in range(2):
                 for kind in range(2):
                     slot = first + e + 4 * kind
-
-                    def rows(b, c2):
-                        at = pl.ds(pl.multiple_of(b * 256, 256), 256)
-                        res[e, kind, at, :] = lax.dot_general(
-                            tabv[side, slot, at, :], ft[side * 8 + slot],
-                            (((1,), (1,)), ((), ())), preferred_element_type=F32,
-                        )
-                        return c2
-
-                    lax.fori_loop(0, DEG // 256, rows, 0)
+                    res[e, kind] = lax.dot_general(
+                        tabv[side, slot], ft[side * 8 + slot],
+                        (((1,), (1,)), ((), ())), preferred_element_type=F32,
+                    )
 
             at32 = lax.broadcasted_iota(jnp.int32, (32, 128), 0)
 
@@ -169,17 +174,32 @@
             return carry
 
         lax.fori_loop(0, 4, two_pairs, 0)
-        for d in range(1, NARROW):
-            to = lax.rem(n + d, NARROW)
-            pltpu.make_async_remote_copy(
-                src_ref=pbuf.at[k, to], dst_ref=brecv.at[k, d - 1],
-                send_sem=b_send.at[k], recv_sem=b_recv.at[k],
-                device_id=(w, to), device_id_type=MESH,
-            ).start()
+        hop(pbuf.at[k, opposite, pl.ds(0, HALF)], bpass.at[k, 0], right, b_send.at[k, 0], b_recv.at[k, 0])
+        hop(pbuf.at[k, opposite, pl.ds(HALF, HALF)], bpass.at[k, 1], left, b_send.at[k, 1], b_recv.at[k, 1])
+        hop(pbuf.at[k, right, pl.ds(HALF, HALF)], brecv.at[k, 0, pl.ds(HALF, HALF)], right, b_send.at[k, 2], b_recv.at[k, 2])
+        hop(pbuf.at[k, left, pl.ds(0, HALF)], brecv.at[k, 1, pl.ds(0, HALF)], left, b_send.at[k, 3], b_recv.at[k, 3])
+
+    def combine(k):
+        for way, (to, base) in enumerate(((right, 0), (left, HALF))):
+            landed(bpass.at[k, way], b_recv.at[k, way])
+
+            def add(t, carry):
+                here = pl.ds(pl.multiple_of(base + t * 96, 32), 96)
+                there = pl.ds(pl.multiple_of(t * 96, 32), 96)
+                pbuf[k, to, here, :] = (
+                    pbuf[k, to, here, :].astype(F32) + bpass[k, way, there, :].astype(F32)
+                ).astype(BF16)
+                return carry
+
+            lax.fori_loop(0, HALF // 96, add, 0)
+            half = pl.ds(base, HALF)
+            hop(pbuf.at[k, to, half], brecv.at[k, way, half], to, b_send.at[k, 4 + way], b_recv.at[k, 4 + way])
 
     def spectral(k):
-        whole = brecv.at[k]
-        pltpu.make_async_copy(whole, whole, b_recv.at[k]).wait()
+        landed(brecv.at[k, 0, pl.ds(HALF, HALF)], b_recv.at[k, 2])
+        landed(brecv.at[k, 1, pl.ds(0, HALF)], b_recv.at[k, 3])
+        landed(brecv.at[k, 0, pl.ds(0, HALF)], b_recv.at[k, 4])
+        landed(brecv.at[k, 1, pl.ds(HALF, HALF)], b_recv.at[k, 5])
 
         def modes_of(kind):
             return jnp.concatenate(
@@ -192,7 +212,7 @@
         def put(pos, v, kind, m):
             rows = pl.ds(pl.multiple_of(pos * 64, 64), 64)
             total = pbuf[k, n, rows, :].astype(F32)
-            for d in range(NARROW - 1):
+            for d in range(2):
                 total = total + brecv[k, d, rows, :].astype(F32)
             turned = jnp.swapaxes(total.reshape(8, 8, 128), 0, 1)
             kept = jnp.where(at + (v * 32 + n * 8) >= m[None], turned, 0.0)
@@ -248,24 +268,23 @@
         transform(k)
         if k:
             spectral(k - 1)
+        combine(k)
     spectral(NCH - 1)
 
-    def drain(ref, sem):
-        pltpu.make_async_copy(ref, ref, sem).wait()
-
     for k in range(NCH):
-        drain(arecv.at[k, pl.ds(0, 15)], a_send.at[k])
-        drain(brecv.at[k], b_send.at[k])
+        landed(arecv.at[k, pl.ds(0, 15)], a_send.at[k])
+        for i in range(6):
+            landed(bpass.at[k, 0], b_send.at[k, i])
 
         @pl.when(w >= WIDE // 2)
         def _():
-            drain(csend.at[k, pl.ds(0, 46)], c_send.at[k])
-            drain(crecv.at[k], c_recv.at[k])
+            landed(csend.at[k, pl.ds(0, 46)], c_send.at[k])
+            landed(crecv.at[k], c_recv.at[k])
 
         @pl.when(w < WIDE // 2)
         def _():
-            drain(csend.at[k, pl.ds(0, 47)], c_send.at[k])
-            drain(crecv.at[k, pl.ds(0, 32)], c_recv.at[k])
+            landed(csend.at[k, pl.ds(0, 47)], c_send.at[k])
+            landed(crecv.at[k, pl.ds(0, 32)], c_recv.at[k])
     inv_out.wait()
 
 
@@ -312,12 +331,13 @@
             pltpu.VMEM((16, 128, TB), BF16),
             pltpu.VMEM((2, 2, DEG, 128), F32),
             pltpu.VMEM((NCH, NARROW, ROWS, 128), BF16),
-            pltpu.VMEM((NCH, NARROW - 1, ROWS, 128), BF16),
+            pltpu.VMEM((NCH, 2, ROWS, 128), BF16),
+            pltpu.VMEM((NCH, 2, HALF, 128), BF16),
             pltpu.VMEM((NCH, 2 * WIDE, 64, 128), BF16),
             pltpu.VMEM((8, 512, 512), BF16),
             pltpu.VMEM((8, 512, 512), BF16),
             pltpu.VMEM((512, 512), BF16),
-            dma((NCH,)), dma((NCH,)), dma((6,)), dma((NCH,)), dma((NCH,)),
+            dma((NCH,)), dma((NCH,)), dma((6,)), dma((NCH, 6)), dma((NCH, 6)),
             dma((NCH,)), dma((NCH,)), dma((2,)),
         ],
         compiler_params=pltpu.CompilerParams(

time: 172 us -> 146 us (0.85); the launches traced: 168 us -> 144 us
  Pallas kernels: 165 us -> 140 us
    pallas_call x1, Pallas kernels: 154 us -> 130 us  [per_device(): pl.pallas_call(transform_kernel, name='transform', out_shape=(jax.ShapeDt...]
where the time goes in v2:
time: 146 us; the launch traced here: 144 us
  Pallas kernels  140 us (96%)
  local copies, waits for them, and re-layouts  3.5 us (2%)
    pallas_call x1, Pallas kernels, per_device(): pl.pallas_call(transform_kernel, name='transform', out_shape=(jax.ShapeDt...  130 us
    pallas_call x1, Pallas kernels, per_device(): pl.pallas_call(solve_kernel, name='solve', out_shape=jax.ShapeDtypeStruct...  10.5 us

profile of v2, /device:TPU:19, one launch (start us, length us, event | category | flops | bytes accessed | tf_op | source)
XLA Modules:
  0.0 143.9 jit_solution(1969119463612083961)
XLA Ops:
  0.0 1.3 broadcast_in_dim.2.modes
  1.3 129.9 %transform.1 = (bf16[4,64,64,128]{3,2,1,0:T(8,128)(2,1)}, bf16[8,512,512]{2,1,0:T(8,128)(2,1)}) custom-call(bf16[16,2,16,16,384]{4,3,2,1,0:T(8,128)(2,1)} %bitcast.4, bf16[8,1024,384]{2,1,0:T(8,128)(2,1)} %table.1, s32[8,128]{1,0:T(8,128)} %broadcast_in_dim.2.modes, bf16[8,512,512]{2,1,0:T(8,128)(2,1)} %inverse.1), custom_call_target="tpu_custom_call" | custom-call | tf_op jit(solution)/shard_map/transform/pallas_call | solution.py:318
  131.2 0.0 copy-start
  131.2 2.2 %copy-done = bf16[4,64,64,128]{3,2,1,0:T(8,128)(2,1)S(1)} copy-done((bf16[4,64,64,128]{3,2,1,0:T(8,128)(2,1)S(1)}, bf16[4,64,64,128]{3,2,1,0:T(8,128)(2,1)}, u32[]{:S(2)}) %copy-start) | copy-done | bytes 4194328
  133.4 10.5 %solve.1 = f32[8,2,256,512]{3,2,1,0:T(8,128)} custom-call(s32[1]{0:T(128)} %bitcast.where, bf16[4,16,2,2,64,128]{5,4,3,2,1,0:T(8,128)(2,1)S(1)} %bitcast.3, bf16[8,512,512]{2,1,0:T(8,128)(2,1)} %get-tuple-element.8.inv_ref), custom_call_target="tpu_custom_call" | custom-call | tf_op jit(solution)/shard_map/solve/pallas_call | solution.py:349
Async XLA Ops:
  131.2 2.2 %copy-start = (bf16[4,64,64,128]{3,2,1,0:T(8,128)(2,1)S(1)}, bf16[4,64,64,128]{3,2,1,0:T(8,128)(2,1)}, u32[]{:S(2)}) copy-start(bf16[4,64,64,128]{3,2,1,0:T(8,128)(2,1)} %get-tuple-element.7) | copy-start | bytes 12582916

commit v3 on v2

--- a/solution.py
+++ b/solution.py
@@ -43,8 +43,8 @@
 
     own_table = pltpu.make_async_copy(table, tabv.at[core], t_sem.at[0])
     own_table.start()
-    own_modes = pltpu.make_async_copy(modes, modv.at[core], t_sem.at[1])
-    own_modes.start()
+    for i in range(8):
+        modv[core, i, :] = jnp.full((128,), modes[i], jnp.int32)
     inv_in = pltpu.make_async_copy(inverse, invv, i_sem.at[0])
     inv_in.start()
     for k in range(NCH):
@@ -69,7 +69,7 @@
 
     def send_field(k):
         for dy, dz in PLANE:
-            peer = lax.rem(y + dy, 4) * 4 + lax.rem(z + dz, 4)
+            peer = lax.rem(y + dy + core * (4 - 2 * dy), 4) * 4 + lax.rem(z + dz + core * (4 - 2 * dz), 4)
             pltpu.make_async_remote_copy(
                 src_ref=field.at[pl.ds(8 * (k % 2), 8), k // 2, peer],
                 dst_ref=arecv.at[k, q],
@@ -80,7 +80,7 @@
             ).start()
 
     give_modes = pltpu.make_async_remote_copy(
-        src_ref=modes, dst_ref=modv.at[core], send_sem=t_sem.at[2],
+        src_ref=modv.at[core], dst_ref=modv.at[core], send_sem=t_sem.at[2],
         recv_sem=t_sem.at[3], device_id=(sib, n), device_id_type=MESH,
     )
     give_modes.start()
@@ -111,7 +111,6 @@
     inv_out.start()
 
     own_table.wait()
-    own_modes.wait()
     give_modes.wait()
     give_table.wait()
 
@@ -209,60 +208,78 @@
         lo_modes, hi_modes = modes_of(0), modes_of(1)
         at = lax.broadcasted_iota(jnp.int32, (8, 8, 128), 0)
 
-        def put(pos, v, kind, m):
+        upper = lax.broadcasted_iota(jnp.int32, (8, 8, 128), 1) < 4
+
+        def total(pos, v, m):
             rows = pl.ds(pl.multiple_of(pos * 64, 64), 64)
-            total = pbuf[k, n, rows, :].astype(F32)
+            vals = pbuf[k, n, rows, :].astype(F32)
             for d in range(2):
-                total = total + brecv[k, d, rows, :].astype(F32)
-            turned = jnp.swapaxes(total.reshape(8, 8, 128), 0, 1)
-            kept = jnp.where(at + (v * 32 + n * 8) >= m[None], turned, 0.0)
-            csend[k, 2 * v + kind] = kept.reshape(64, 128).astype(BF16)
+                vals = vals + brecv[k, d, rows, :].astype(F32)
+            turned = jnp.swapaxes(vals.reshape(8, 8, 128), 0, 1)
+            return jnp.where(at + (v * 32 + n * 8) >= m[None], turned, 0.0)
 
         def low(v, carry):
-            put(v + 1, v, 0, lo_modes)
+            csend[k, v, pl.ds(0, 64), :] = total(v + 1, v, lo_modes).reshape(64, 128).astype(BF16)
             return carry
 
         def high(v, carry):
-            put(31 - v, v, 1, hi_modes)
-            return carry
-
-        lax.fori_loop(0, WIDE, low, 0)
+            lo = total(v + 1, v, lo_modes)
+            hi = total(31 - v, v, hi_modes)
+            first = jnp.where(upper, lo, pltpu.roll(hi, 4, 1))
+            second = jnp.where(upper, pltpu.roll(lo, 4, 1), hi)
+            both = jnp.concatenate([first, second], axis=1).reshape(128, 128)
+            csend[k, v] = both.astype(BF16)
+            return carry
+
+        lax.fori_loop(0, WIDE // 2, low, 0)
         lax.fori_loop(WIDE // 2, WIDE, high, 0)
 
+        target = crecv.at[k, q, core]
+
+        def keep(count):
+            pltpu.make_async_copy(
+                csend.at[k, w, pl.ds(0, count)], target.at[pl.ds(0, count)], c_recv.at[k]
+            ).start()
+
         @pl.when(w >= WIDE // 2)
         def _():
-            pltpu.make_async_copy(
-                csend.at[k, pl.ds(2 * w, 2)], crecv.at[k, pl.ds(2 * w, 2)], c_recv.at[k]
-            ).start()
+            keep(128)
 
         @pl.when(w < WIDE // 2)
         def _():
-            pltpu.make_async_copy(
-                csend.at[k, pl.ds(2 * w, 1)], crecv.at[k, pl.ds(2 * w, 1)], c_recv.at[k]
-            ).start()
+            keep(64)
 
         def give(t, carry):
-            to = lax.rem(w + t, WIDE)
+            to = lax.rem(w + 11 * t, WIDE)
 
             def go(count):
                 pltpu.make_async_remote_copy(
-                    src_ref=csend.at[k, pl.ds(2 * to, count)],
-                    dst_ref=crecv.at[k, pl.ds(2 * w, count)],
+                    src_ref=csend.at[k, to, pl.ds(0, count)],
+                    dst_ref=target.at[pl.ds(0, count)],
                     send_sem=c_send.at[k], recv_sem=c_recv.at[k],
                     device_id=(to, n), device_id_type=MESH,
                 ).start()
 
             @pl.when(to >= WIDE // 2)
             def _():
-                go(2)
+                go(128)
 
             @pl.when(to < WIDE // 2)
             def _():
-                go(1)
+                go(64)
 
             return carry
 
         lax.fori_loop(1, WIDE, give, 0)
+
+    def received(k):
+        @pl.when(w >= WIDE // 2)
+        def _():
+            landed(crecv.at[k], c_recv.at[k])
+
+        @pl.when(w < WIDE // 2)
+        def _():
+            landed(crecv.at[k, :, :, pl.ds(0, 64)], c_recv.at[k])
 
     for k in range(NCH):
         transform(k)
@@ -270,6 +287,8 @@
             spectral(k - 1)
         combine(k)
     spectral(NCH - 1)
+    for k in range(NCH):
+        received(k)
 
     for k in range(NCH):
         landed(arecv.at[k, pl.ds(0, 15)], a_send.at[k])
@@ -278,51 +297,97 @@
 
         @pl.when(w >= WIDE // 2)
         def _():
-            landed(csend.at[k, pl.ds(0, 46)], c_send.at[k])
-            landed(crecv.at[k], c_recv.at[k])
+            landed(csend.at[k, pl.ds(0, 23)], c_send.at[k])
 
         @pl.when(w < WIDE // 2)
         def _():
-            landed(csend.at[k, pl.ds(0, 47)], c_send.at[k])
-            landed(crecv.at[k, pl.ds(0, 32)], c_recv.at[k])
+            landed(csend.at[k, pl.ds(0, 23)], c_send.at[k])
+            landed(csend.at[k, 0, pl.ds(0, 64)], c_send.at[k])
     inv_out.wait()
 
 
-def solve_kernel(where, x_ref, inv_ref, out_ref):
-    keep = where[0] >= WIDE // 2
-    vals = x_ref[...].astype(F32)
-    lane = vals.reshape(2, CHIPS, 2, 2, 2, 8, 128)
-    for e in range(2):
-        blocks = []
-        for half in range(2):
-            for g in range(2):
-                lo = lane[g, :, half, 0, e]
-                hi = jnp.where(keep, lane[g, :, half, 1, e], 0.0)
-                both = jnp.stack([lo, hi], axis=1)
-                blocks.append(both.reshape(CHIPS * 16, 128).astype(BF16))
-        lhs = jnp.concatenate(blocks, axis=1)
-        got = jnp.dot(lhs, inv_ref[e], preferred_element_type=F32)
-        got = got.reshape(CHIPS, 2, 8, 512)
-        lo, hi = got[:, 0], got[:, 1]
-        first = jnp.concatenate([lo[:, :4], hi[:, :4]], axis=1)
-        second = jnp.concatenate([lo[:, 4:], hi[:, 4:]], axis=1)
-        out_ref[e, 0] = jnp.stack([first, second], axis=1).reshape(256, 512)
+def solve_upper(x, inv, c, t):
+    rows = pl.ds(pl.multiple_of(t * 16, 16), 16)
+    blocks = [
+        x[2 * c + g, :, half, rows, :].reshape(CHIPS * 16, 128)
+        for half in range(2) for g in range(2)
+    ]
+    return jnp.dot(jnp.concatenate(blocks, axis=1), inv[t], preferred_element_type=F32)
+
+
+def solve_lower(x, inv, c, t):
+    rows = pl.ds(pl.multiple_of((t // 2) * 16, 16), 16)
+    even = lax.broadcasted_iota(jnp.int32, (CHIPS, 8, 128), 1) * 0 + t % 2 == 0
+    blocks = []
+    for half in range(2):
+        for g in range(2):
+            two = x[2 * c + g, :, half, rows, :].astype(F32)
+            one = jnp.where(even, two[:, :8], two[:, 8:])
+            blocks.append(one.reshape(CHIPS * 8, 128).astype(BF16))
+    got = jnp.dot(
+        jnp.concatenate(blocks, axis=1), inv[t], preferred_element_type=F32
+    ).reshape(CHIPS, 8, 512)
+    upper = lax.broadcasted_iota(jnp.int32, (CHIPS, 8, 512), 1) < 4
+    first = jnp.where(upper, got, 0.0)
+    second = jnp.where(upper, pltpu.roll(got, 4, 1), 0.0)
+    return jnp.concatenate([first, second], axis=1).reshape(256, 512)
+
+
+def solve_kernel(where, x, inv, solved, xv, invv, outv, x_sem, i_sem, o_sem):
+    def run(rows, solve):
+        copies = [
+            pltpu.make_async_copy(
+                x.at[k, :, half, pl.ds(0, rows)], xv.at[k, :, half, pl.ds(0, rows)],
+                x_sem.at[k, half],
+            )
+            for k in range(NCH) for half in range(2)
+        ]
+        for copy in copies[:4]:
+            copy.start()
+
+        def fetch(t, carry):
+            pltpu.make_async_copy(inv.at[t], invv.at[t], i_sem.at[t]).start()
+            return carry
+
+        lax.fori_loop(0, 8, fetch, 0)
+        for copy in copies[4:]:
+            copy.start()
+        for c in range(2):
+            for copy in copies[4 * c:4 * c + 4]:
+                copy.wait()
+
+            def degree(t, carry):
+                if c == 0:
+                    pltpu.make_async_copy(inv.at[t], invv.at[t], i_sem.at[t]).wait()
+                outv[c, t] = solve(xv, invv, c, t)
+                pltpu.make_async_copy(outv.at[c, t], solved.at[t, c], o_sem).start()
+                return carry
+
+            lax.fori_loop(0, 8, degree, 0)
+
+    @pl.when(where[0] >= WIDE // 2)
+    def _():
+        run(128, solve_upper)
+
+    @pl.when(where[0] < WIDE // 2)
+    def _():
+        run(64, solve_lower)
+
+    pltpu.make_async_copy(outv, outv, o_sem).wait()
 
 
 def per_device(field, table, inverse, modes):
     fields = field.reshape(16, 2, CHIPS, 16, TB)
-    modes_rows = jnp.broadcast_to(modes[:, None], (8, 128))
     any_spec = pl.BlockSpec(memory_space=pl.ANY)
-    vmem_spec = pl.BlockSpec(memory_space=pltpu.VMEM)
     dma = pltpu.SemaphoreType.DMA
     crecv, invt = pl.pallas_call(
         transform_kernel,
         name="transform",
         out_shape=(
-            jax.ShapeDtypeStruct((NCH, 2 * WIDE, 64, 128), BF16),
+            jax.ShapeDtypeStruct((NCH, CHIPS, 2, 128, 128), BF16),
             jax.ShapeDtypeStruct((8, 512, 512), BF16),
         ),
-        in_specs=[any_spec, any_spec, vmem_spec, any_spec],
+        in_specs=[any_spec, any_spec, pl.BlockSpec(memory_space=pltpu.SMEM), any_spec],
         out_specs=(any_spec, any_spec),
         scratch_shapes=[
             pltpu.VMEM((NCH, CHIPS, 8, 16, TB), BF16),
@@ -333,7 +398,7 @@
             pltpu.VMEM((NCH, NARROW, ROWS, 128), BF16),
             pltpu.VMEM((NCH, 2, ROWS, 128), BF16),
             pltpu.VMEM((NCH, 2, HALF, 128), BF16),
-            pltpu.VMEM((NCH, 2 * WIDE, 64, 128), BF16),
+            pltpu.VMEM((NCH, WIDE, 128, 128), BF16),
             pltpu.VMEM((8, 512, 512), BF16),
             pltpu.VMEM((8, 512, 512), BF16),
             pltpu.VMEM((512, 512), BF16),
@@ -343,24 +408,22 @@
         compiler_params=pltpu.CompilerParams(
             collective_id=0, has_side_effects=True, vmem_limit_bytes=60 * 2**20
         ),
-    )(fields, table, modes_rows, inverse)
-    x = crecv.reshape(NCH, CHIPS, 2, 2, 64, 128)
+    )(fields, table, modes, inverse)
     where = lax.axis_index("wide").astype(jnp.int32).reshape(1)
     return pl.pallas_call(
         solve_kernel,
         name="solve",
         out_shape=jax.ShapeDtypeStruct((8, 2, 256, 512), F32),
-        grid_spec=pltpu.PrefetchScalarGridSpec(
-            num_scalar_prefetch=1,
-            grid=(4, 2),
-            in_specs=[
-                pl.BlockSpec((2, CHIPS, 2, 2, 16, 128), lambda i, c, s: (c, 0, 0, 0, i, 0)),
-                pl.BlockSpec((2, 512, 512), lambda i, c, s: (i, 0, 0)),
-            ],
-            out_specs=pl.BlockSpec((2, 1, 256, 512), lambda i, c, s: (i, c, 0, 0)),
-        ),
-        compiler_params=pltpu.CompilerParams(vmem_limit_bytes=48 * 2**20),
-    )(where, x, invt)
+        in_specs=[pl.BlockSpec(memory_space=pltpu.SMEM), any_spec, any_spec],
+        out_specs=any_spec,
+        scratch_shapes=[
+            pltpu.VMEM((NCH, CHIPS, 2, 128, 128), BF16),
+            pltpu.VMEM((8, 512, 512), BF16),
+            pltpu.VMEM((2, 8, 256, 512), F32),
+            dma((NCH, 2)), dma((8,)), dma(()),
+        ],
+        compiler_params=pltpu.CompilerParams(vmem_limit_bytes=60 * 2**20),
+    )(where, crecv, invt)
 
 
 def solution(mesh):

time: 146 us -> 132 us (0.904)
  Pallas kernels: 140 us -> 130 us
  local copies, waits for them, and re-layouts: 3.5 us -> 0 us
    pallas_call x1, Pallas kernels: 130 us -> 123 us  [per_device(): pl.pallas_call(transform_kernel, name='transform', out_shape=(jax.ShapeDt...]
    pallas_call x1, Pallas kernels: 10.5 us -> 7.56 us  [per_device(): pl.pallas_call(solve_kernel, name='solve', out_shape=jax.ShapeDtypeStruct...]
    unnamed x2 -> x0, local copies, waits for them, and re-layouts: 2.18 us -> none
where the time goes in v3:
time: 132 us; the launch traced here: 130 us
  Pallas kernels  130 us (98%)
    pallas_call x1, Pallas kernels, per_device(): pl.pallas_call(transform_kernel, name='transform', out_shape=(jax.ShapeDt...  123 us
    pallas_call x1, Pallas kernels, per_device(): pl.pallas_call(solve_kernel, name='solve', out_shape=jax.ShapeDtypeStruct...  7.56 us

profile of v3, /device:TPU:19, one launch (start us, length us, event | category | flops | bytes accessed | tf_op | source)
XLA Modules:
  0.0 130.3 jit_solution(17754482911914315082)
XLA Ops:
  0.0 122.7 %transform.1 = (bf16[4,16,2,128,128]{4,3,2,1,0:T(8,128)(2,1)}, bf16[8,512,512]{2,1,0:T(8,128)(2,1)}) custom-call(bf16[16,2,16,16,384]{4,3,2,1,0:T(8,128)(2,1)} %bitcast.2, bf16[8,1024,384]{2,1,0:T(8,128)(2,1)} %table.1, s32[8]{0:T(128)} %modes.1, bf16[8,512,512]{2,1,0:T(8,128)(2,1)} %inverse.1), custom_call_target="tpu_custom_call" | custom-call | tf_op jit(solution)/shard_map/transform/pallas_call | solution.py:383
  122.7 7.6 %solve.1 = f32[8,2,256,512]{3,2,1,0:T(8,128)} custom-call(s32[1]{0:T(128)} %bitcast.where, bf16[4,16,2,128,128]{4,3,2,1,0:T(8,128)(2,1)} %get-tuple-element.7.x, bf16[8,512,512]{2,1,0:T(8,128)(2,1)} %get-tuple-element.8.inv), custom_call_target="tpu_custom_call" | custom-call | tf_op jit(solution)/shard_map/solve/pallas_call | solution.py:413

commit v4 on v3

--- a/solution.py
+++ b/solution.py
@@ -21,10 +21,7 @@
 NCH = 4
 TB = 384
 
-PLANE = [
-    (0, 1), (1, 0), (0, 3), (3, 0), (1, 1), (3, 3), (1, 3), (3, 1),
-    (0, 2), (2, 0), (1, 2), (2, 1), (3, 2), (2, 3), (2, 2),
-]
+PLANE = [(1, 1), (2, 2), (3, 3), (0, 1), (1, 2), (2, 3), (3, 0), (0, 2), (1, 3), (2, 0), (3, 1), (0, 3), (1, 0), (2, 1), (3, 2)]
 
 
 def transform_kernel(
@@ -250,7 +247,13 @@
             keep(64)
 
         def give(t, carry):
-            to = lax.rem(w + 11 * t, WIDE)
+            u, c2 = t % 16, t // 16
+            dy, dz = u % 4, (u // 4 + u) % 4
+            to = (
+                lax.rem(y + dy + core * (4 - 2 * dy), 4) * 8
+                + lax.rem(z + dz + core * (4 - 2 * dz), 4) * 2
+                + lax.rem(core + c2, 2)
+            )
 
             def go(count):
                 pltpu.make_async_remote_copy(
@@ -306,31 +309,35 @@
     inv_out.wait()
 
 
-def solve_upper(x, inv, c, t):
+def solve_upper(x, inv, t):
     rows = pl.ds(pl.multiple_of(t * 16, 16), 16)
     blocks = [
-        x[2 * c + g, :, half, rows, :].reshape(CHIPS * 16, 128)
+        jnp.concatenate([x[2 * c + g, :, half, rows, :].reshape(CHIPS * 16, 128) for c in range(2)], axis=0)
         for half in range(2) for g in range(2)
     ]
-    return jnp.dot(jnp.concatenate(blocks, axis=1), inv[t], preferred_element_type=F32)
-
-
-def solve_lower(x, inv, c, t):
+    got = jnp.dot(jnp.concatenate(blocks, axis=1), inv[t], preferred_element_type=F32)
+    return got.reshape(2, 256, 512)
+
+
+def solve_lower(x, inv, t):
     rows = pl.ds(pl.multiple_of((t // 2) * 16, 16), 16)
     even = lax.broadcasted_iota(jnp.int32, (CHIPS, 8, 128), 1) * 0 + t % 2 == 0
     blocks = []
     for half in range(2):
         for g in range(2):
-            two = x[2 * c + g, :, half, rows, :].astype(F32)
-            one = jnp.where(even, two[:, :8], two[:, 8:])
-            blocks.append(one.reshape(CHIPS * 8, 128).astype(BF16))
+            both = []
+            for c in range(2):
+                two = x[2 * c + g, :, half, rows, :].astype(F32)
+                one = jnp.where(even, two[:, :8], two[:, 8:])
+                both.append(one.reshape(CHIPS * 8, 128).astype(BF16))
+            blocks.append(jnp.concatenate(both, axis=0))
     got = jnp.dot(
         jnp.concatenate(blocks, axis=1), inv[t], preferred_element_type=F32
-    ).reshape(CHIPS, 8, 512)
-    upper = lax.broadcasted_iota(jnp.int32, (CHIPS, 8, 512), 1) < 4
+    ).reshape(2 * CHIPS, 8, 512)
+    upper = lax.broadcasted_iota(jnp.int32, (2 * CHIPS, 8, 512), 1) < 4
     first = jnp.where(upper, got, 0.0)
     second = jnp.where(upper, pltpu.roll(got, 4, 1), 0.0)
-    return jnp.concatenate([first, second], axis=1).reshape(256, 512)
+    return jnp.concatenate([first, second], axis=1).reshape(2, 256, 512)
 
 
 def solve_kernel(where, x, inv, solved, xv, invv, outv, x_sem, i_sem, o_sem):
@@ -342,28 +349,24 @@
             )
             for k in range(NCH) for half in range(2)
         ]
-        for copy in copies[:4]:
-            copy.start()
 
         def fetch(t, carry):
             pltpu.make_async_copy(inv.at[t], invv.at[t], i_sem.at[t]).start()
             return carry
 
+        for copy in copies:
+            copy.start()
         lax.fori_loop(0, 8, fetch, 0)
-        for copy in copies[4:]:
-            copy.start()
-        for c in range(2):
-            for copy in copies[4 * c:4 * c + 4]:
-                copy.wait()
-
-            def degree(t, carry):
-                if c == 0:
-                    pltpu.make_async_copy(inv.at[t], invv.at[t], i_sem.at[t]).wait()
-                outv[c, t] = solve(xv, invv, c, t)
-                pltpu.make_async_copy(outv.at[c, t], solved.at[t, c], o_sem).start()
-                return carry
-
-            lax.fori_loop(0, 8, degree, 0)
+        for copy in copies:
+            copy.wait()
+
+        def degree(t, carry):
+            pltpu.make_async_copy(inv.at[t], invv.at[t], i_sem.at[t]).wait()
+            outv[t] = solve(xv, invv, t)
+            pltpu.make_async_copy(outv.at[t], solved.at[t], o_sem).start()
+            return carry
+
+        lax.fori_loop(0, 8, degree, 0)
 
     @pl.when(where[0] >= WIDE // 2)
     def _():
@@ -419,7 +422,7 @@
         scratch_shapes=[
             pltpu.VMEM((NCH, CHIPS, 2, 128, 128), BF16),
             pltpu.VMEM((8, 512, 512), BF16),
-            pltpu.VMEM((2, 8, 256, 512), F32),
+            pltpu.VMEM((8, 2, 256, 512), F32),
             dma((NCH, 2)), dma((8,)), dma(()),
         ],
         compiler_params=pltpu.CompilerParams(vmem_limit_bytes=60 * 2**20),

time: 132 us -> 132 us (level)
    pallas_call x1, Pallas kernels: 123 us -> 125 us  [per_device(): pl.pallas_call(transform_kernel, name='transform', out_shape=(jax.ShapeDt...]
where the time goes in v4:
time: 132 us; the launch traced here: 131 us
  Pallas kernels  131 us (99%)
    pallas_call x1, Pallas kernels, per_device(): pl.pallas_call(transform_kernel, name='transform', out_shape=(jax.ShapeDt...  125 us
    pallas_call x1, Pallas kernels, per_device(): pl.pallas_call(solve_kernel, name='solve', out_shape=jax.ShapeDtypeStruct...  6.96 us

profile of v4, /device:TPU:19, one launch (start us, length us, event | category | flops | bytes accessed | tf_op | source)
XLA Modules:
  0.0 131.5 jit_solution(10284736739381855514)
XLA Ops:
  0.0 124.5 %transform.1 = (bf16[4,16,2,128,128]{4,3,2,1,0:T(8,128)(2,1)}, bf16[8,512,512]{2,1,0:T(8,128)(2,1)}) custom-call(bf16[16,2,16,16,384]{4,3,2,1,0:T(8,128)(2,1)} %bitcast.2, bf16[8,1024,384]{2,1,0:T(8,128)(2,1)} %table.1, s32[8]{0:T(128)} %modes.1, bf16[8,512,512]{2,1,0:T(8,128)(2,1)} %inverse.1), custom_call_target="tpu_custom_call" | custom-call | tf_op jit(solution)/shard_map/transform/pallas_call | solution.py:386
  124.5 7.0 %solve.1 = f32[8,2,256,512]{3,2,1,0:T(8,128)} custom-call(s32[1]{0:T(128)} %bitcast.where, bf16[4,16,2,128,128]{4,3,2,1,0:T(8,128)(2,1)} %get-tuple-element.7.x, bf16[8,512,512]{2,1,0:T(8,128)(2,1)} %get-tuple-element.8.inv), custom_call_target="tpu_custom_call" | custom-call | tf_op jit(solution)/shard_map/solve/pallas_call | solution.py:416

commit v5 on v4

--- a/solution.py
+++ b/solution.py
@@ -216,7 +216,8 @@
             return jnp.where(at + (v * 32 + n * 8) >= m[None], turned, 0.0)
 
         def low(v, carry):
-            csend[k, v, pl.ds(0, 64), :] = total(v + 1, v, lo_modes).reshape(64, 128).astype(BF16)
+            lo = total(v + 1, v, lo_modes).reshape(4, 16, 128)
+            csend[k, v, :, pl.ds(0, 16), :] = lo.astype(BF16)
             return carry
 
         def high(v, carry):
@@ -224,27 +225,27 @@
             hi = total(31 - v, v, hi_modes)
             first = jnp.where(upper, lo, pltpu.roll(hi, 4, 1))
             second = jnp.where(upper, pltpu.roll(lo, 4, 1), hi)
-            both = jnp.concatenate([first, second], axis=1).reshape(128, 128)
+            both = jnp.concatenate([first, second], axis=1).reshape(4, 32, 128)
             csend[k, v] = both.astype(BF16)
             return carry
 
         lax.fori_loop(0, WIDE // 2, low, 0)
         lax.fori_loop(WIDE // 2, WIDE, high, 0)
 
-        target = crecv.at[k, q, core]
+        target = crecv.at[:, k, q, core]
 
         def keep(count):
             pltpu.make_async_copy(
-                csend.at[k, w, pl.ds(0, count)], target.at[pl.ds(0, count)], c_recv.at[k]
+                csend.at[k, w, :, pl.ds(0, count)], target.at[:, pl.ds(0, count)], c_recv.at[k]
             ).start()
 
         @pl.when(w >= WIDE // 2)
         def _():
-            keep(128)
+            keep(32)
 
         @pl.when(w < WIDE // 2)
         def _():
-            keep(64)
+            keep(16)
 
         def give(t, carry):
             u, c2 = t % 16, t // 16
@@ -257,19 +258,19 @@
 
             def go(count):
                 pltpu.make_async_remote_copy(
-                    src_ref=csend.at[k, to, pl.ds(0, count)],
-                    dst_ref=target.at[pl.ds(0, count)],
+                    src_ref=csend.at[k, to, :, pl.ds(0, count)],
+                    dst_ref=target.at[:, pl.ds(0, count)],
                     send_sem=c_send.at[k], recv_sem=c_recv.at[k],
                     device_id=(to, n), device_id_type=MESH,
                 ).start()
 
             @pl.when(to >= WIDE // 2)
             def _():
-                go(128)
+                go(32)
 
             @pl.when(to < WIDE // 2)
             def _():
-                go(64)
+                go(16)
 
             return carry
 
@@ -278,11 +279,11 @@
     def received(k):
         @pl.when(w >= WIDE // 2)
         def _():
-            landed(crecv.at[k], c_recv.at[k])
+            landed(crecv.at[:, k], c_recv.at[k])
 
         @pl.when(w < WIDE // 2)
         def _():
-            landed(crecv.at[k, :, :, pl.ds(0, 64)], c_recv.at[k])
+            landed(crecv.at[:, k, :, :, pl.ds(0, 16)], c_recv.at[k])
 
     for k in range(NCH):
         transform(k)
@@ -305,34 +306,38 @@
         @pl.when(w < WIDE // 2)
         def _():
             landed(csend.at[k, pl.ds(0, 23)], c_send.at[k])
-            landed(csend.at[k, 0, pl.ds(0, 64)], c_send.at[k])
+            landed(csend.at[k, 0, :, pl.ds(0, 16)], c_send.at[k])
     inv_out.wait()
 
 
-def solve_upper(x, inv, t):
-    rows = pl.ds(pl.multiple_of(t * 16, 16), 16)
+def solve_upper(x, inv, pair, e):
     blocks = [
-        jnp.concatenate([x[2 * c + g, :, half, rows, :].reshape(CHIPS * 16, 128) for c in range(2)], axis=0)
+        jnp.concatenate(
+            [
+                x[pair, 2 * c + g, :, half, 16 * e:16 * e + 16, :].reshape(CHIPS * 16, 128)
+                for c in range(2)
+            ],
+            axis=0,
+        )
         for half in range(2) for g in range(2)
     ]
-    got = jnp.dot(jnp.concatenate(blocks, axis=1), inv[t], preferred_element_type=F32)
+    got = jnp.dot(
+        jnp.concatenate(blocks, axis=1), inv[2 * pair + e], preferred_element_type=F32
+    )
     return got.reshape(2, 256, 512)
 
 
-def solve_lower(x, inv, t):
-    rows = pl.ds(pl.multiple_of((t // 2) * 16, 16), 16)
-    even = lax.broadcasted_iota(jnp.int32, (CHIPS, 8, 128), 1) * 0 + t % 2 == 0
+def solve_lower(x, inv, pair, e):
     blocks = []
     for half in range(2):
         for g in range(2):
             both = []
             for c in range(2):
-                two = x[2 * c + g, :, half, rows, :].astype(F32)
-                one = jnp.where(even, two[:, :8], two[:, 8:])
-                both.append(one.reshape(CHIPS * 8, 128).astype(BF16))
+                two = x[pair, 2 * c + g, :, half, 0:16, :].astype(F32)
+                both.append(two[:, 8 * e:8 * e + 8].reshape(CHIPS * 8, 128).astype(BF16))
             blocks.append(jnp.concatenate(both, axis=0))
     got = jnp.dot(
-        jnp.concatenate(blocks, axis=1), inv[t], preferred_element_type=F32
+        jnp.concatenate(blocks, axis=1), inv[2 * pair + e], preferred_element_type=F32
     ).reshape(2 * CHIPS, 8, 512)
     upper = lax.broadcasted_iota(jnp.int32, (2 * CHIPS, 8, 512), 1) < 4
     first = jnp.where(upper, got, 0.0)
@@ -342,39 +347,39 @@
 
 def solve_kernel(where, x, inv, solved, xv, invv, outv, x_sem, i_sem, o_sem):
     def run(rows, solve):
-        copies = [
-            pltpu.make_async_copy(
-                x.at[k, :, half, pl.ds(0, rows)], xv.at[k, :, half, pl.ds(0, rows)],
-                x_sem.at[k, half],
-            )
-            for k in range(NCH) for half in range(2)
-        ]
-
-        def fetch(t, carry):
-            pltpu.make_async_copy(inv.at[t], invv.at[t], i_sem.at[t]).start()
-            return carry
-
-        for copy in copies:
-            copy.start()
-        lax.fori_loop(0, 8, fetch, 0)
-        for copy in copies:
-            copy.wait()
-
-        def degree(t, carry):
-            pltpu.make_async_copy(inv.at[t], invv.at[t], i_sem.at[t]).wait()
-            outv[t] = solve(xv, invv, t)
-            pltpu.make_async_copy(outv.at[t], solved.at[t], o_sem).start()
-            return carry
-
-        lax.fori_loop(0, 8, degree, 0)
+        def rows_of(pair):
+            part = (pair, slice(None), slice(None), slice(None), pl.ds(0, rows))
+            return pltpu.make_async_copy(x.at[part], xv.at[part], x_sem.at[pair])
+
+        def inverse_of(t):
+            return pltpu.make_async_copy(inv.at[t], invv.at[t], i_sem.at[t])
+
+        def fetch(pair, carry):
+            rows_of(pair).start()
+            inverse_of(2 * pair).start()
+            inverse_of(2 * pair + 1).start()
+            return carry
+
+        lax.fori_loop(0, 4, fetch, 0)
+
+        def degrees(pair, carry):
+            rows_of(pair).wait()
+            for e in range(2):
+                t = 2 * pair + e
+                inverse_of(t).wait()
+                outv[t] = solve(xv, invv, pair, e)
+                pltpu.make_async_copy(outv.at[t], solved.at[t], o_sem).start()
+            return carry
+
+        lax.fori_loop(0, 4, degrees, 0)
 
     @pl.when(where[0] >= WIDE // 2)
     def _():
-        run(128, solve_upper)
+        run(32, solve_upper)
 
     @pl.when(where[0] < WIDE // 2)
     def _():
-        run(64, solve_lower)
+        run(16, solve_lower)
 
     pltpu.make_async_copy(outv, outv, o_sem).wait()
 
@@ -387,7 +392,7 @@
         transform_kernel,
         name="transform",
         out_shape=(
-            jax.ShapeDtypeStruct((NCH, CHIPS, 2, 128, 128), BF16),
+            jax.ShapeDtypeStruct((4, NCH, CHIPS, 2, 32, 128), BF16),
             jax.ShapeDtypeStruct((8, 512, 512), BF16),
         ),
         in_specs=[any_spec, any_spec, pl.BlockSpec(memory_space=pltpu.SMEM), any_spec],
@@ -401,7 +406,7 @@
             pltpu.VMEM((NCH, NARROW, ROWS, 128), BF16),
             pltpu.VMEM((NCH, 2, ROWS, 128), BF16),
             pltpu.VMEM((NCH, 2, HALF, 128), BF16),
-            pltpu.VMEM((NCH, WIDE, 128, 128), BF16),
+            pltpu.VMEM((NCH, WIDE, 4, 32, 128), BF16),
             pltpu.VMEM((8, 512, 512), BF16),
             pltpu.VMEM((8, 512, 512), BF16),
             pltpu.VMEM((512, 512), BF16),
@@ -420,10 +425,10 @@
         in_specs=[pl.BlockSpec(memory_space=pltpu.SMEM), any_spec, any_spec],
         out_specs=any_spec,
         scratch_shapes=[
-            pltpu.VMEM((NCH, CHIPS, 2, 128, 128), BF16),
+            pltpu.VMEM((4, NCH, CHIPS, 2, 32, 128), BF16),
             pltpu.VMEM((8, 512, 512), BF16),
             pltpu.VMEM((8, 2, 256, 512), F32),
-            dma((NCH, 2)), dma((8,)), dma(()),
+            dma((4,)), dma((8,)), dma(()),
         ],
         compiler_params=pltpu.CompilerParams(vmem_limit_bytes=60 * 2**20),
     )(where, crecv, invt)

time: 132 us -> 131 us (level)
  no operation moved by 1% of the time
where the time goes in v5:
time: 131 us
  Pallas kernels  131 us (100%)
    pallas_call x1, Pallas kernels, per_device(): pl.pallas_call(transform_kernel, name='transform', out_shape=(jax.ShapeDt...  125 us
    pallas_call x1, Pallas kernels, per_device(): pl.pallas_call(solve_kernel, name='solve', out_shape=jax.ShapeDtypeStruct...  6.47 us

profile of v5, /device:TPU:19, one launch (start us, length us, event | category | flops | bytes accessed | tf_op | source)
XLA Modules:
  0.0 131.0 jit_solution(13700623342513220440)
XLA Ops:
  0.0 124.5 %transform.1 = (bf16[4,4,16,2,32,128]{5,4,3,2,1,0:T(8,128)(2,1)}, bf16[8,512,512]{2,1,0:T(8,128)(2,1)}) custom-call(bf16[16,2,16,16,384]{4,3,2,1,0:T(8,128)(2,1)} %bitcast.2, bf16[8,1024,384]{2,1,0:T(8,128)(2,1)} %table.1, s32[8]{0:T(128)} %modes.1, bf16[8,512,512]{2,1,0:T(8,128)(2,1)} %inverse.1), custom_call_target="tpu_custom_call" | custom-call | tf_op jit(solution)/shard_map/transform/pallas_call | solution.py:391
  124.5 6.5 %solve.1 = f32[8,2,256,512]{3,2,1,0:T(8,128)} custom-call(s32[1]{0:T(128)} %bitcast.where, bf16[4,4,16,2,32,128]{5,4,3,2,1,0:T(8,128)(2,1)} %get-tuple-element.7.x, bf16[8,512,512]{2,1,0:T(8,128)(2,1)} %get-tuple-element.8.inv), custom_call_target="tpu_custom_call" | custom-call | tf_op jit(solution)/shard_map/solve/pallas_call | solution.py:421

commit v6 on v5

--- a/solution.py
+++ b/solution.py
@@ -248,12 +248,10 @@
             keep(16)
 
         def give(t, carry):
-            u, c2 = t % 16, t // 16
-            dy, dz = u % 4, (u // 4 + u) % 4
+            u = lax.rem(t, 16)
             to = (
-                lax.rem(y + dy + core * (4 - 2 * dy), 4) * 8
-                + lax.rem(z + dz + core * (4 - 2 * dz), 4) * 2
-                + lax.rem(core + c2, 2)
+                16 - 16 * (t // 16) + 8 * lax.rem(y + u, 2) + 2 * lax.rem(z + u // 2, 4)
+                + lax.rem(core + u // 8, 2)
             )
 
             def go(count):
@@ -264,17 +262,17 @@
                     device_id=(to, n), device_id_type=MESH,
                 ).start()
 
-            @pl.when(to >= WIDE // 2)
+            @pl.when((to >= WIDE // 2) & (to != w))
             def _():
                 go(32)
 
-            @pl.when(to < WIDE // 2)
+            @pl.when((to < WIDE // 2) & (to != w))
             def _():
                 go(16)
 
             return carry
 
-        lax.fori_loop(1, WIDE, give, 0)
+        lax.fori_loop(0, WIDE, give, 0)
 
     def received(k):
         @pl.when(w >= WIDE // 2)
@@ -368,7 +366,8 @@
                 t = 2 * pair + e
                 inverse_of(t).wait()
                 outv[t] = solve(xv, invv, pair, e)
-                pltpu.make_async_copy(outv.at[t], solved.at[t], o_sem).start()
+                for c in range(2):
+                    pltpu.make_async_copy(outv.at[t, c], solved.at[t, c], o_sem).start()
             return carry
 
         lax.fori_loop(0, 4, degrees, 0)

time: 131 us -> 130 us (level)
  no operation moved by 1% of the time
where the time goes in v6:
time: 130 us
  Pallas kernels  130 us (100%)
    pallas_call x1, Pallas kernels, per_device(): pl.pallas_call(transform_kernel, name='transform', out_shape=(jax.ShapeDt...  124 us
    pallas_call x1, Pallas kernels, per_device(): pl.pallas_call(solve_kernel, name='solve', out_shape=jax.ShapeDtypeStruct...  6.45 us

profile of v6, /device:TPU:19, one launch (start us, length us, event | category | flops | bytes accessed | tf_op | source)
XLA Modules:
  0.0 130.2 jit_solution(9977478947949955249)
XLA Ops:
  0.0 123.8 %transform.1 = (bf16[4,4,16,2,32,128]{5,4,3,2,1,0:T(8,128)(2,1)}, bf16[8,512,512]{2,1,0:T(8,128)(2,1)}) custom-call(bf16[16,2,16,16,384]{4,3,2,1,0:T(8,128)(2,1)} %bitcast.2, bf16[8,1024,384]{2,1,0:T(8,128)(2,1)} %table.1, s32[8]{0:T(128)} %modes.1, bf16[8,512,512]{2,1,0:T(8,128)(2,1)} %inverse.1), custom_call_target="tpu_custom_call" | custom-call | tf_op jit(solution)/shard_map/transform/pallas_call | solution.py:390
  123.8 6.4 %solve.1 = f32[8,2,256,512]{3,2,1,0:T(8,128)} custom-call(s32[1]{0:T(128)} %bitcast.where, bf16[4,4,16,2,32,128]{5,4,3,2,1,0:T(8,128)(2,1)} %get-tuple-element.7.x, bf16[8,512,512]{2,1,0:T(8,128)(2,1)} %get-tuple-element.8.inv), custom_call_target="tpu_custom_call" | custom-call | tf_op jit(solution)/shard_map/solve/pallas_call | solution.py:420

commit v7 on v6

--- a/solution.py
+++ b/solution.py
@@ -38,6 +38,19 @@
     z = q % 4
     sib = w + 1 - 2 * core
 
+    barrier = pltpu.get_barrier_semaphore()
+
+    def greet(t, carry):
+        pl.semaphore_signal(
+            barrier, inc=1, device_id=(lax.rem(w + t, WIDE), n), device_id_type=MESH
+        )
+        return carry
+
+    lax.fori_loop(1, WIDE, greet, 0)
+    for d in range(1, NARROW):
+        pl.semaphore_signal(
+            barrier, inc=1, device_id=(w, lax.rem(n + d, NARROW)), device_id_type=MESH
+        )
     own_table = pltpu.make_async_copy(table, tabv.at[core], t_sem.at[0])
     own_table.start()
     for i in range(8):
@@ -49,19 +62,6 @@
             field.at[pl.ds(8 * (k % 2), 8), k // 2, q], arecv.at[k, q], a_recv.at[k]
         ).start()
 
-    barrier = pltpu.get_barrier_semaphore()
-
-    def greet(t, carry):
-        pl.semaphore_signal(
-            barrier, inc=1, device_id=(lax.rem(w + t, WIDE), n), device_id_type=MESH
-        )
-        return carry
-
-    lax.fori_loop(1, WIDE, greet, 0)
-    for d in range(1, NARROW):
-        pl.semaphore_signal(
-            barrier, inc=1, device_id=(w, lax.rem(n + d, NARROW)), device_id_type=MESH
-        )
     pl.semaphore_wait(barrier, WIDE - 1 + NARROW - 1)
 
     def send_field(k):

time: 130 us -> 130 us (level)
  no operation moved by 1% of the time
where the time goes in v7:
time: 130 us
  Pallas kernels  130 us (100%)
    pallas_call x1, Pallas kernels, per_device(): pl.pallas_call(transform_kernel, name='transform', out_shape=(jax.ShapeDt...  124 us
    pallas_call x1, Pallas kernels, per_device(): pl.pallas_call(solve_kernel, name='solve', out_shape=jax.ShapeDtypeStruct...  6.45 us

profile of v7, /device:TPU:19, one launch (start us, length us, event | category | flops | bytes accessed | tf_op | source)
XLA Modules:
  0.0 130.2 jit_solution(13472768283582184118)
XLA Ops:
  0.0 123.8 %transform.1 = (bf16[4,4,16,2,32,128]{5,4,3,2,1,0:T(8,128)(2,1)}, bf16[8,512,512]{2,1,0:T(8,128)(2,1)}) custom-call(bf16[16,2,16,16,384]{4,3,2,1,0:T(8,128)(2,1)} %bitcast.2, bf16[8,1024,384]{2,1,0:T(8,128)(2,1)} %table.1, s32[8]{0:T(128)} %modes.1, bf16[8,512,512]{2,1,0:T(8,128)(2,1)} %inverse.1), custom_call_target="tpu_custom_call" | custom-call | tf_op jit(solution)/shard_map/transform/pallas_call | solution.py:390
  123.8 6.4 %solve.1 = f32[8,2,256,512]{3,2,1,0:T(8,128)} custom-call(s32[1]{0:T(128)} %bitcast.where, bf16[4,4,16,2,32,128]{5,4,3,2,1,0:T(8,128)(2,1)} %get-tuple-element.7.x, bf16[8,512,512]{2,1,0:T(8,128)(2,1)} %get-tuple-element.8.inv), custom_call_target="tpu_custom_call" | custom-call | tf_op jit(solution)/shard_map/solve/pallas_call | solution.py:420
